TPU v7x, 768 devices: a whole 4x8x12 slice. The times are simulated.
768 devices in a mesh: dp: 96 (over z, x, core), group: 8 (over y).
Axes of the slice: x: 4, y: 8, z: 12, core: 2. Of those that a mesh axis runs over, the one named last changes fastest.
Arguments:
- partials: bfloat16 [96, 2304, 2048], P('dp', None, 'group')
- momentum: float32 [2304, 2048], P('dp', 'group'), may hold values from -6 to 6
Outputs:
- update: float32 [2304, 2048], P('dp', 'group')
- new_momentum: float32 [2304, 2048], P('dp', 'group')
All inputs are finite; a program needn't handle non-finite values.
Results may differ from a plain program's by a relative error of at most 0.0003.
Values sent between devices are 32-bit elements; how exact they have to be, the bound alone decides.
No kernel may reach another device: no remote copies, remote signals or barrier semaphores. Data moves between devices by JAX's collectives and lax.ppermute only.
A program may use at most 32 MiB of HBM per device.

v0:
```python
import functools
import math

import jax
import jax.numpy as jnp
import numpy as np
from jax import lax
from jax.experimental import pallas as pl
from jax.experimental.pallas import tpu as pltpu
from jax.sharding import Mesh
from jax.sharding import PartitionSpec as P

D = 2048
KV_ROWS = 576
MATS = 4
PADDED = 640
TILE = 128

coef_a = 3.4445
coef_b = -4.775
coef_c = 2.0315

GAIN = 1.95
KAPPA = 0.9025 / 1.95

BLOCK = 64

STRIPS = [((0, 0), (8, 8))]
STRIPS += [
    ((i, 2 * j), (i, 2 * j + 1))
    for i in range(1, 9)
    for j in range(i // 2 + 1)
    if (i, j) != (8, 4)
]
STARTS = [next(n for n, (a, _) in enumerate(STRIPS) if a[0] == i) for i in range(9)]
PAIRS = [(i, j) for i in range(5) for j in range(i + 1)]

CHUNKS = 4
SEND_LIMIT = 54788096

VMEM = pl.BlockSpec(memory_space=pltpu.VMEM)
HBM = pl.BlockSpec(memory_space=pltpu.HBM)
NT = (((1,), (1,)), ((), ()))
NN = (((1,), (0,)), ((), ()))


def place():
    w, v, x, c = (lax.axis_index(name) for name in ("w", "v", "x", "c"))
    first = (((3 * w + v) * 4 + x) * 2 + c) * 24
    return c, first, 48 * v + 12 * x + 6 * c, c * 12 + v * 4 + x


def sort_chunk(q, first, own_rows, wide, out_ref):
    chunk = wide.shape[0] // CHUNKS

    @pl.when(first // chunk == q)
    def _():
        wide[pl.ds(pl.multiple_of(first, 8), 24), :] += KAPPA * own_rows

    for m in range(MATS):
        rows = pl.ds(q * chunk + m, chunk // MATS, stride=MATS)
        groups = slice(q * 12 // CHUNKS, (q + 1) * 12 // CHUNKS)
        out_ref[groups, m] = wide[rows, :].reshape(-1, 48, TILE)


def send_kernel(partial_ref, held, out_ref, raw, wide, sems):
    core, first = place()[:2]
    chunk = raw.shape[0] // CHUNKS
    columns = pl.ds(pl.multiple_of((1 - core) * TILE, TILE), TILE)
    copies = []
    for q in range(CHUNKS):
        rows = pl.ds(q * chunk, chunk)
        copies.append(
            pltpu.make_async_copy(partial_ref.at[rows, columns], raw.at[rows], sems.at[q])
        )
    for copy in copies:
        copy.start()
    own_rows = held[:, columns]
    for q in range(CHUNKS):
        copies[q].wait()
        rows = slice(q * chunk, (q + 1) * chunk)
        wide[rows, :] = raw[rows, :].astype(jnp.float32)
        sort_chunk(q, first, own_rows, wide, out_ref)


def keep_kernel(raw, held, out_ref, wide):
    core, first = place()[:2]
    chunk = raw.shape[0] // CHUNKS
    columns = pl.ds(pl.multiple_of(core * TILE, TILE), TILE)
    own_rows = held[:, columns]
    for q in range(CHUNKS):
        rows = slice(q * chunk, (q + 1) * chunk)
        wide[rows, :] = raw[rows, columns].astype(jnp.float32)
        sort_chunk(q, first, own_rows, wide, out_ref)


HALF = jax.ShapeDtypeStruct((12, MATS, 48, TILE), jnp.float32)
WIDE = pltpu.VMEM((MATS * KV_ROWS, TILE), jnp.float32)
COST = pl.CostEstimate(flops=1 << 20, bytes_accessed=3 << 20, transcendentals=0)


def to_send(partial, momentum):
    return pl.pallas_call(
        send_kernel,
        out_shape=HALF,
        in_specs=[HBM, VMEM],
        out_specs=VMEM,
        scratch_shapes=[
            pltpu.VMEM((MATS * KV_ROWS, TILE), jnp.bfloat16),
            WIDE,
            pltpu.SemaphoreType.DMA((CHUNKS,)),
        ],
        compiler_params=pltpu.CompilerParams(vmem_limit_bytes=SEND_LIMIT),
        cost_estimate=COST,
    )(partial, momentum)


def to_keep(partial, momentum):
    return pl.pallas_call(
        keep_kernel,
        out_shape=HALF,
        in_specs=[VMEM, VMEM],
        out_specs=VMEM,
        scratch_shapes=[WIDE],
        compiler_params=pltpu.CompilerParams(vmem_limit_bytes=16 << 20),
        cost_estimate=COST,
    )(partial, momentum)


def gram_kernel(halves_ref, out_ref):
    strip = place()[3]
    i, start = jnp.int32(0), jnp.int32(0)
    for begin, step in zip(STARTS[1:], np.diff(STARTS)):
        past = strip >= begin
        i += past.astype(jnp.int32)
        start += jnp.where(past, int(step), 0)
    j = 2 * (strip - start)
    ends = strip == 0
    sides = [(i, j), (jnp.where(ends, 8, i), jnp.where(ends, 8, j + 1))]
    for side, pair in enumerate(sides):
        picks = [pl.ds(pl.multiple_of(k * BLOCK, BLOCK), BLOCK) for k in pair]
        left, right = (
            jnp.concatenate([halves_ref[0, rows, :], halves_ref[1, rows, :]], 1) for rows in picks
        )
        out_ref[:, side * BLOCK : (side + 1) * BLOCK] = lax.dot_general(
            left,
            right,
            NT,
            precision=lax.Precision.HIGHEST,
            preferred_element_type=jnp.float32,
        )


def gram(halves):
    return pl.pallas_call(
        gram_kernel,
        out_shape=jax.ShapeDtypeStruct((BLOCK, TILE), jnp.float32),
        in_specs=[VMEM],
        out_specs=VMEM,
        compiler_params=pltpu.CompilerParams(vmem_limit_bytes=24 << 20),
    )(halves)


def three(x):
    top = x.astype(jnp.bfloat16)
    rest = x - top.astype(jnp.float32)
    middle = rest.astype(jnp.bfloat16)
    bottom = (rest - middle.astype(jnp.float32)).astype(jnp.bfloat16)
    return top, middle, bottom


def times(x, right):
    n = x.shape[0]
    parts = three(x)
    total = 0.0
    for at, ref in reversed(list(enumerate(right))):
        product = lax.dot_general(
            jnp.concatenate(parts[: 3 - at], 0),
            ref[...],
            NN,
            preferred_element_type=jnp.float32,
        )
        for k in reversed(range(3 - at)):
            total = total + product[k * n : (k + 1) * n]
    return total


def triangle(strips_ref):
    zero = jnp.zeros((BLOCK, BLOCK), jnp.float32)
    strip = {}
    for at, ((i, j), other) in enumerate(STRIPS[1:], 1):
        strip[i, j // 2] = strips_ref[at]
    ends = strips_ref[0]
    strip[0, 0] = jnp.concatenate([ends[:, :BLOCK], strip[1, 0][:, :BLOCK].T], 1)
    strip[8, 4] = jnp.concatenate([ends[:, BLOCK:], zero], 1)
    blank = jnp.concatenate([zero, zero], 1)
    return {
        (i, j): jnp.concatenate([strip[2 * i, j], strip.get((2 * i + 1, j), blank)], 0)
        for i, j in PAIRS
    }


def chain_kernel(strips_ref, halves_ref, out_ref, g0, g1, t0, t1, t2):
    first_row = place()[2]
    blocks = triangle(strips_ref)
    row = lax.broadcasted_iota(jnp.int32, (TILE, TILE), 0)
    column = lax.broadcasted_iota(jnp.int32, (TILE, TILE), 1)
    diagonal = jnp.zeros((TILE, TILE), jnp.float32)
    for i in range(5):
        diagonal += jnp.where(row == column, blocks[i, i], 0.0)
    squares = jnp.sum(jnp.sum(diagonal, axis=0, keepdims=True), axis=1, keepdims=True)
    scale = GAIN / (GAIN * jnp.sqrt(squares) + 1e-07)
    for i, j in PAIRS:
        block = (blocks[i, j] * scale) * scale
        here = (slice(i * TILE, (i + 1) * TILE), slice(j * TILE, (j + 1) * TILE))
        for ref, part in zip((g0, g1), three(block)):
            ref[here] = part
        if i != j:
            for ref, part in zip((g0, g1), three(block.T)):
                ref[here[1], here[0]] = part
    for half in range(2):
        for ref, part in zip((t0, t1, t2), three(halves_ref[half])):
            ref[:KV_ROWS, half * TILE : (half + 1) * TILE] = part
    for ref in (t0, t1, t2):
        ref[KV_ROWS:, :] = jnp.zeros((PADDED - KV_ROWS, 2 * TILE), jnp.bfloat16)
    g, t = (g0, g1), (t0, t1, t2)

    r = lax.broadcasted_iota(jnp.int32, (32, PADDED), 0)
    k = lax.broadcasted_iota(jnp.int32, (32, PADDED), 1)
    wanted = first_row + 144 * (r >> 3) + (r & 7)
    pick = jnp.where(jnp.logical_and(k == wanted, (r & 7) < 6), 1.0, 0.0)

    def poly(x):
        once = times(x, g)
        return coef_a * x + coef_b * once + coef_c * times(once, g)

    first = poly(pick)
    second = times(poly(poly(first)), g)
    third = times(poly(poly(second)), g)
    rows = coef_a * first + coef_b * second + coef_c * third
    gain = (0.2 * math.sqrt(max(KV_ROWS, D))) * scale
    both = times(jnp.concatenate([rows, pick], 0), t)
    update, own = gain * both[:32], both[32:]
    for x in range(4):
        out_ref[x, :8, :] = update[8 * x : 8 * x + 8]
        out_ref[x, 8:, :] = own[8 * x : 8 * x + 8]


def chain(strips, halves):
    return pl.pallas_call(
        chain_kernel,
        out_shape=jax.ShapeDtypeStruct((4, 16, 2 * TILE), jnp.float32),
        in_specs=[VMEM, VMEM],
        out_specs=VMEM,
        scratch_shapes=[pltpu.VMEM((PADDED, PADDED), jnp.bfloat16)] * 2
        + [pltpu.VMEM((PADDED, 2 * TILE), jnp.bfloat16)] * 3,
        compiler_params=pltpu.CompilerParams(vmem_limit_bytes=24 << 20),
    )(strips, halves)


def finish_kernel(got_ref, momentum_ref, update_ref, new_ref, update_half, sum_half):
    for half in range(2):
        columns = slice(half * TILE, (half + 1) * TILE)
        for m in range(MATS):
            rows = pl.ds(m, 6, stride=MATS)
            update_half[rows, :] = got_ref[m, 0:6, columns]
            sum_half[rows, :] = got_ref[m, 8:14, columns]
        momentum = momentum_ref[:, columns]
        update_ref[:, columns] = update_half[...]
        new_ref[:, columns] = 0.95 * momentum + (sum_half[...] - KAPPA * momentum)


def finish(got, momentum):
    shape = jax.ShapeDtypeStruct(momentum.shape, jnp.float32)
    return pl.pallas_call(
        finish_kernel,
        out_shape=(shape, shape),
        in_specs=[VMEM, VMEM],
        out_specs=(VMEM, VMEM),
        scratch_shapes=[pltpu.VMEM((24, TILE), jnp.float32)] * 2,
        compiler_params=pltpu.CompilerParams(vmem_limit_bytes=4 << 20),
    )(got, momentum)


def exchange(x, axis):
    return lax.all_to_all(x, axis, split_axis=0, concat_axis=0, tiled=True)


def spread(x, axis, count):
    return exchange(jnp.broadcast_to(x[None], (count, *x.shape)), axis)


def per_device(partials, momentum):
    send = to_send(partials[0], momentum)
    got = lax.ppermute(send, "c", [(0, 1), (1, 0)])
    keep = to_keep(partials[0], momentum)
    near = jnp.sum(exchange(keep + got, ("v", "x")), axis=0)
    own = jnp.sum(exchange(near, "w"), axis=0)
    half = spread(own, ("v", "x"), 12).reshape(KV_ROWS, TILE)
    halves = lax.all_gather(half, "c", axis=0, tiled=False)
    mine = jnp.sum(spread(gram(halves), "y", 8), axis=0)
    strips = lax.all_gather(spread(mine, ("v", "x"), 12), "c", axis=0, tiled=True)
    done = chain(strips, halves)
    return finish(exchange(done, "w"), momentum)


def solution(mesh):
    fine = Mesh(mesh.devices.reshape(4, 3, 4, 2, 8), ("w", "v", "x", "c", "y"))
    rows = ("w", "v", "x", "c")
    return jax.shard_map(
        per_device,
        mesh=fine,
        in_specs=(P(rows, None, "y"), P(rows, "y")),
        out_specs=(P(rows, "y"), P(rows, "y")),
        check_vma=False,
    )
```

profile of v0, /device:TPU:1, one launch (start us, length us, event | category | flops | bytes accessed | tf_op | source)
XLA Modules:
  0.0 131.4 jit_solution(13035875882302956141)
XLA Ops:
  0.6 0.0 copy-start.1
  0.6 0.7 copy-done.1
  1.4 0.0 copy-start
  1.4 1.3 shard_map.42
  2.7 12.4 %collective-permute-start = (f32[12,4,48,128]{3,2,1,0:T(8,128)S(1)}, f32[12,4,48,128]{3,2,1,0:T(8,128)S(1)}, u32[]{:S(2)}, u32[]{:S(2)}) collective-permute-start(f32[12,4,48,128]{3,2,1,0:T(8,128)S(1)} %shard_map.42), channel_id=1, source_target_pairs={{0,8},{8,0},{1,9},{9,1},{2,10},{10,2},{3,11},{11,3},{4,12},{12,4},... | collective-permute-start | bytes 3538952 | tf_op jit(solution)/shard_map/ppermute | solution.py:295
  15.1 0.0 copy-done
  15.1 0.2 shard_map.41
  15.3 2.2 %collective-permute-done = f32[12,4,48,128]{3,2,1,0:T(8,128)S(1)} collective-permute-done((f32[12,4,48,128]{3,2,1,0:T(8,128)S(1)}, f32[12,4,48,128]{3,2,1,0:T(8,128)S(1)}, u32[]{:S(2)}, u32[]{:S(2)}) %collective-permute-start) | collective-permute-done | bytes 1179680 | tf_op jit(solution)/shard_map/ppermute | solution.py:295
  17.6 0.1 add.3
  17.7 22.1 %all_to_all.30 = f32[12,4,48,128]{3,2,1,0:T(8,128)S(1)} all-to-all(f32[12,4,48,128]{3,2,1,0:T(8,128)S(1)} %add.3), channel_id=1, replica_groups=mesh['w'=4,'v'=3,'x'=4,'c'=2,'y'=8] {'v','x'}, dimensions={0} | all-to-all | bytes 2359296 | tf_op jit(solution)/shard_map/all_to_all | solution.py:286
  39.8 0.1 reduce_sum.27
  39.8 18.8 %all_to_all.31 = f32[4,48,128]{2,1,0:T(8,128)S(1)} all-to-all(f32[4,48,128]{2,1,0:T(8,128)S(1)} %reduce_sum.27), channel_id=1, replica_groups=mesh['w'=4,'v'=3,'x'=4,'c'=2,'y'=8] {'w'}, dimensions={0} | all-to-all | bytes 196608 | tf_op jit(solution)/shard_map/all_to_all | solution.py:286
  58.7 11.9 %all_to_all.32 = f32[12,48,128]{2,1,0:T(8,128)S(1)} all-to-all(f32[12,48,128]{2,1,0:T(8,128)S(1)} %broadcast_in_dim.6), channel_id=1, replica_groups=mesh['w'=4,'v'=3,'x'=4,'c'=2,'y'=8] {'v','x'}, dimensions={0} | all-to-all | bytes 589824 | tf_op jit(solution)/shard_map/all_to_all | solution.py:286
  70.6 6.3 %all_gather.6.halves_ref = f32[2,576,128]{2,1,0:T(8,128)S(1)} all-gather(f32[1,576,128]{2,1,0:T(8,128)S(1)} %bitcast.4), channel_id=1, replica_groups=mesh['w'=4,'v'=3,'x'=4,'c'=2,'y'=8] {'c'}, dimensions={0}, use_global_device_ids=true | all-gather | bytes 884736 | tf_op jit(solution)/shard_map/all_gather | solution.py:300
  76.8 0.3 shard_map.43
  77.2 17.7 %all_to_all.33 = f32[8,64,128]{2,1,0:T(8,128)S(1)} all-to-all(f32[8,64,128]{2,1,0:T(8,128)S(1)} %broadcast_in_dim.7), channel_id=1, replica_groups=mesh['w'=4,'v'=3,'x'=4,'c'=2,'y'=8] {'y'}, dimensions={0} | all-to-all | bytes 524288 | tf_op jit(solution)/shard_map/all_to_all | solution.py:286
  94.9 10.5 %all_to_all.34 = f32[12,64,128]{2,1,0:T(8,128)S(1)} all-to-all(f32[12,64,128]{2,1,0:T(8,128)S(1)} %broadcast_in_dim.8), channel_id=1, replica_groups=mesh['w'=4,'v'=3,'x'=4,'c'=2,'y'=8] {'v','x'}, dimensions={0} | all-to-all | bytes 786432 | tf_op jit(solution)/shard_map/all_to_all | solution.py:286
  105.5 0.0 copy-start.2
  105.5 5.5 %all_gather.7.strips_ref = f32[24,64,128]{2,1,0:T(8,128)S(1)} all-gather(f32[12,64,128]{2,1,0:T(8,128)S(1)} %all_to_all.34), channel_id=1, replica_groups=mesh['w'=4,'v'=3,'x'=4,'c'=2,'y'=8] {'c'}, dimensions={0}, use_global_device_ids=true | all-gather | bytes 1179648 | tf_op jit(solution)/shard_map/all_gather | solution.py:302
  110.9 5.4 %shard_map.44 = f32[4,16,256]{2,1,0:T(8,128)S(1)} custom-call(f32[24,64,128]{2,1,0:T(8,128)S(1)} %all_gather.7.strips_ref, f32[2,576,128]{2,1,0:T(8,128)S(1)} %all_gather.6.halves_ref), custom_call_target="tpu_custom_call" | custom-call | tf_op jit(solution)/shard_map/pallas_call | solution.py:250
  116.4 14.4 %all_to_all.35.got_ref = f32[4,16,256]{2,1,0:T(8,128)S(1)} all-to-all(f32[4,16,256]{2,1,0:T(8,128)S(1)} %shard_map.44), channel_id=1, replica_groups=mesh['w'=4,'v'=3,'x'=4,'c'=2,'y'=8] {'w'}, dimensions={0} | all-to-all | bytes 131072 | tf_op jit(solution)/shard_map/all_to_all | solution.py:286
  130.7 0.0 copy-done.2
  130.7 0.6 shard_map.45
  (5 shorter events, 0.1 us)
Async XLA Ops:
  0.6 0.7 copy-start.1
  1.4 13.7 %copy-start = (bf16[1,2304,256]{2,1,0:T(8,128)(2,1)S(1)}, bf16[1,2304,256]{2,1,0:T(8,128)(2,1)}, u32[]{:S(2)}) copy-start(bf16[1,2304,256]{2,1,0:T(8,128)(2,1)} %param.2) | copy-start | bytes 3538948
  2.7 14.9 %collective-permute-start = (f32[12,4,48,128]{3,2,1,0:T(8,128)S(1)}, f32[12,4,48,128]{3,2,1,0:T(8,128)S(1)}, u32[]{:S(2)}, u32[]{:S(2)}) collective-permute-start(f32[12,4,48,128]{3,2,1,0:T(8,128)S(1)} %shard_map.42), channel_id=1, source_target_pairs={{0,8},{8,0},{1,9},{9,1},{2,10},{10,2},{3,11},{11,3},{4,12},{12,4},... | collective-permute-start | bytes 3538952 | tf_op jit(solution)/shard_map/ppermute | solution.py:295
  105.5 25.3 %copy-start.2 = (f32[24,256]{1,0:T(8,128)S(1)}, f32[24,256]{1,0:T(8,128)}, u32[]{:S(2)}) copy-start(f32[24,256]{1,0:T(8,128)} %momentum_ref.1) | copy-start | bytes 73732
where the time goes:
time: 132 us; the launch traced here: 131 us
  blocking collectives  107 us (81%)
  starting transfers between devices  12.4 us (9%)
  Pallas kernels  7.87 us (6%)
  waiting for transfers between devices  2.25 us (2%)
    all_to_all x6, blocking collectives, exchange(): return lax.all_to_all(x, axis, split_axis=0, concat_axis=0, tiled=True)  95.3 us
    ppermute x1, starting transfers between devices, per_device(): got = lax.ppermute(send, 'c', [(0, 1), (1, 0)])  12.4 us
    all_gather x1, blocking collectives, per_device(): halves = lax.all_gather(half, 'c', axis=0, tiled=False)  6.28 us
    all_gather x1, blocking collectives, per_device(): lax.all_gather(spread(mine, ('v', 'x'), 12), 'c', axis=0, tiled=True)  5.47 us
    pallas_call x1, Pallas kernels, chain(): pl.pallas_call(chain_kernel, out_shape=jax.ShapeDtypeStruct((4, 16, 2 * T...  5.44 us
  transfers between devices with their start and end apart: 1, of which 1 were waited for; matrix products, arithmetic and copies ran while one was open for 0% of the time, Pallas kernels for 0%

commit v1 on v0

--- a/solution.py
+++ b/solution.py
@@ -53,9 +53,11 @@
 def sort_chunk(q, first, own_rows, wide, out_ref):
     chunk = wide.shape[0] // CHUNKS
 
-    @pl.when(first // chunk == q)
-    def _():
-        wide[pl.ds(pl.multiple_of(first, 8), 24), :] += KAPPA * own_rows
+    if own_rows is not None:
+
+        @pl.when(first // chunk == q)
+        def _():
+            wide[pl.ds(pl.multiple_of(first, 8), 24), :] += KAPPA * own_rows
 
     for m in range(MATS):
         rows = pl.ds(q * chunk + m, chunk // MATS, stride=MATS)
@@ -63,7 +65,7 @@
         out_ref[groups, m] = wide[rows, :].reshape(-1, 48, TILE)
 
 
-def send_kernel(partial_ref, held, out_ref, raw, wide, sems):
+def send_kernel(partial_ref, out_ref, raw, wide, sems):
     core, first = place()[:2]
     chunk = raw.shape[0] // CHUNKS
     columns = pl.ds(pl.multiple_of((1 - core) * TILE, TILE), TILE)
@@ -75,12 +77,25 @@
         )
     for copy in copies:
         copy.start()
-    own_rows = held[:, columns]
     for q in range(CHUNKS):
         copies[q].wait()
         rows = slice(q * chunk, (q + 1) * chunk)
         wide[rows, :] = raw[rows, :].astype(jnp.float32)
-        sort_chunk(q, first, own_rows, wide, out_ref)
+        sort_chunk(q, first, None, wide, out_ref)
+
+
+def momentum_kernel(held, half_ref, out_ref):
+    core, first = place()[:2]
+    own = first // MATS
+    group, start = own // 48, own % 48
+    rows = KAPPA * held[:, pl.ds(pl.multiple_of((1 - core) * TILE, TILE), TILE)]
+    at = lax.broadcasted_iota(jnp.int32, (48, TILE), 0) - start
+    out_ref[...] = half_ref[...]
+    for m in range(MATS):
+        total = jnp.zeros((48, TILE), jnp.float32)
+        for j in range(6):
+            total = jnp.where(at == j, rows[MATS * j + m : MATS * j + m + 1, :], total)
+        out_ref[group, m] += total
 
 
 def keep_kernel(raw, held, out_ref, wide):
@@ -100,10 +115,10 @@
 
 
 def to_send(partial, momentum):
-    return pl.pallas_call(
+    half = pl.pallas_call(
         send_kernel,
         out_shape=HALF,
-        in_specs=[HBM, VMEM],
+        in_specs=[HBM],
         out_specs=VMEM,
         scratch_shapes=[
             pltpu.VMEM((MATS * KV_ROWS, TILE), jnp.bfloat16),
@@ -112,7 +127,14 @@
         ],
         compiler_params=pltpu.CompilerParams(vmem_limit_bytes=SEND_LIMIT),
         cost_estimate=COST,
-    )(partial, momentum)
+    )(partial)
+    return pl.pallas_call(
+        momentum_kernel,
+        out_shape=HALF,
+        in_specs=[VMEM, VMEM],
+        out_specs=VMEM,
+        compiler_params=pltpu.CompilerParams(vmem_limit_bytes=8 << 20),
+    )(momentum, half)
 
 
 def to_keep(partial, momentum):

time: 132 us -> 131 us (level)
  no operation moved by 1% of the time
where the time goes in v1:
time: 131 us
  blocking collectives  107 us (82%)
  starting transfers between devices  12.6 us (10%)
  Pallas kernels  7.89 us (6%)
  waiting for transfers between devices  2.25 us (2%)
    all_to_all x6, blocking collectives, exchange(): return lax.all_to_all(x, axis, split_axis=0, concat_axis=0, tiled=True)  95.3 us
    ppermute x1, starting transfers between devices, per_device(): got = lax.ppermute(send, 'c', [(0, 1), (1, 0)])  12.6 us
    all_gather x1, blocking collectives, per_device(): halves = lax.all_gather(half, 'c', axis=0, tiled=False)  6.28 us
    pallas_call x1, Pallas kernels, chain(): pl.pallas_call(chain_kernel, out_shape=jax.ShapeDtypeStruct((4, 16, 2 * T...  5.44 us
    all_gather x1, blocking collectives, per_device(): lax.all_gather(spread(mine, ('v', 'x'), 12), 'c', axis=0, tiled=True)  5.34 us
  transfers between devices with their start and end apart: 1, of which 1 were waited for; matrix products, arithmetic and copies ran while one was open for 0% of the time, Pallas kernels for 0%

profile of v1, /device:TPU:1, one launch (start us, length us, event | category | flops | bytes accessed | tf_op | source)
XLA Modules:
  0.0 130.7 jit_solution(7675205605650972996)
XLA Ops:
  0.6 0.0 copy-start.1
  0.6 1.2 shard_map.42.half_ref
  1.9 0.0 copy-done.1
  1.9 0.0 copy-start
  1.9 0.1 shard_map.43
  2.0 12.6 %collective-permute-start = (f32[12,4,48,128]{3,2,1,0:T(8,128)S(1)}, f32[12,4,48,128]{3,2,1,0:T(8,128)S(1)}, u32[]{:S(2)}, u32[]{:S(2)}) collective-permute-start(f32[12,4,48,128]{3,2,1,0:T(8,128)S(1)} %shard_map.43), channel_id=1, source_target_pairs={{0,8},{8,0},{1,9},{9,1},{2,10},{10,2},{3,11},{11,3},{4,12},{12,4},... | collective-permute-start | bytes 3538952 | tf_op jit(solution)/shard_map/ppermute | solution.py:317
  14.6 0.0 copy-done
  14.6 0.2 shard_map.41
  14.8 2.2 %collective-permute-done = f32[12,4,48,128]{3,2,1,0:T(8,128)S(1)} collective-permute-done((f32[12,4,48,128]{3,2,1,0:T(8,128)S(1)}, f32[12,4,48,128]{3,2,1,0:T(8,128)S(1)}, u32[]{:S(2)}, u32[]{:S(2)}) %collective-permute-start) | collective-permute-done | bytes 1179680 | tf_op jit(solution)/shard_map/ppermute | solution.py:317
  17.0 0.1 add.3
  17.2 22.1 %all_to_all.30 = f32[12,4,48,128]{3,2,1,0:T(8,128)S(1)} all-to-all(f32[12,4,48,128]{3,2,1,0:T(8,128)S(1)} %add.3), channel_id=1, replica_groups=mesh['w'=4,'v'=3,'x'=4,'c'=2,'y'=8] {'v','x'}, dimensions={0} | all-to-all | bytes 2359296 | tf_op jit(solution)/shard_map/all_to_all | solution.py:308
  39.2 0.1 reduce_sum.27
  39.3 18.8 %all_to_all.31 = f32[4,48,128]{2,1,0:T(8,128)S(1)} all-to-all(f32[4,48,128]{2,1,0:T(8,128)S(1)} %reduce_sum.27), channel_id=1, replica_groups=mesh['w'=4,'v'=3,'x'=4,'c'=2,'y'=8] {'w'}, dimensions={0} | all-to-all | bytes 196608 | tf_op jit(solution)/shard_map/all_to_all | solution.py:308
  58.2 11.9 %all_to_all.32 = f32[12,48,128]{2,1,0:T(8,128)S(1)} all-to-all(f32[12,48,128]{2,1,0:T(8,128)S(1)} %broadcast_in_dim.6), channel_id=1, replica_groups=mesh['w'=4,'v'=3,'x'=4,'c'=2,'y'=8] {'v','x'}, dimensions={0} | all-to-all | bytes 589824 | tf_op jit(solution)/shard_map/all_to_all | solution.py:308
  70.0 6.3 %all_gather.6.halves_ref = f32[2,576,128]{2,1,0:T(8,128)S(1)} all-gather(f32[1,576,128]{2,1,0:T(8,128)S(1)} %bitcast.4), channel_id=1, replica_groups=mesh['w'=4,'v'=3,'x'=4,'c'=2,'y'=8] {'c'}, dimensions={0}, use_global_device_ids=true | all-gather | bytes 884736 | tf_op jit(solution)/shard_map/all_gather | solution.py:322
  76.3 0.3 shard_map.44
  76.6 17.7 %all_to_all.33 = f32[8,64,128]{2,1,0:T(8,128)S(1)} all-to-all(f32[8,64,128]{2,1,0:T(8,128)S(1)} %broadcast_in_dim.7), channel_id=1, replica_groups=mesh['w'=4,'v'=3,'x'=4,'c'=2,'y'=8] {'y'}, dimensions={0} | all-to-all | bytes 524288 | tf_op jit(solution)/shard_map/all_to_all | solution.py:308
  94.4 10.5 %all_to_all.34 = f32[12,64,128]{2,1,0:T(8,128)S(1)} all-to-all(f32[12,64,128]{2,1,0:T(8,128)S(1)} %broadcast_in_dim.8), channel_id=1, replica_groups=mesh['w'=4,'v'=3,'x'=4,'c'=2,'y'=8] {'v','x'}, dimensions={0} | all-to-all | bytes 786432 | tf_op jit(solution)/shard_map/all_to_all | solution.py:308
  105.0 5.3 %all_gather.7.strips_ref = f32[24,64,128]{2,1,0:T(8,128)S(1)} all-gather(f32[12,64,128]{2,1,0:T(8,128)S(1)} %all_to_all.34), channel_id=1, replica_groups=mesh['w'=4,'v'=3,'x'=4,'c'=2,'y'=8] {'c'}, dimensions={0}, use_global_device_ids=true | all-gather | bytes 1179648 | tf_op jit(solution)/shard_map/all_gather | solution.py:324
  110.3 5.4 %shard_map.45 = f32[4,16,256]{2,1,0:T(8,128)S(1)} custom-call(f32[24,64,128]{2,1,0:T(8,128)S(1)} %all_gather.7.strips_ref, f32[2,576,128]{2,1,0:T(8,128)S(1)} %all_gather.6.halves_ref), custom_call_target="tpu_custom_call" | custom-call | tf_op jit(solution)/shard_map/pallas_call | solution.py:272
  115.7 14.3 %all_to_all.35.got_ref = f32[4,16,256]{2,1,0:T(8,128)S(1)} all-to-all(f32[4,16,256]{2,1,0:T(8,128)S(1)} %shard_map.45), channel_id=1, replica_groups=mesh['w'=4,'v'=3,'x'=4,'c'=2,'y'=8] {'w'}, dimensions={0} | all-to-all | bytes 131072 | tf_op jit(solution)/shard_map/all_to_all | solution.py:308
  130.1 0.6 shard_map.46
  (5 shorter events, 0.1 us)
Async XLA Ops:
  0.6 1.2 copy-start.1
  1.9 12.7 %copy-start = (bf16[1,2304,256]{2,1,0:T(8,128)(2,1)S(1)}, bf16[1,2304,256]{2,1,0:T(8,128)(2,1)}, u32[]{:S(2)}) copy-start(bf16[1,2304,256]{2,1,0:T(8,128)(2,1)} %param.2) | copy-start | bytes 3538948
  2.0 15.0 %collective-permute-start = (f32[12,4,48,128]{3,2,1,0:T(8,128)S(1)}, f32[12,4,48,128]{3,2,1,0:T(8,128)S(1)}, u32[]{:S(2)}, u32[]{:S(2)}) collective-permute-start(f32[12,4,48,128]{3,2,1,0:T(8,128)S(1)} %shard_map.43), channel_id=1, source_target_pairs={{0,8},{8,0},{1,9},{9,1},{2,10},{10,2},{3,11},{11,3},{4,12},{12,4},... | collective-permute-start | bytes 3538952 | tf_op jit(solution)/shard_map/ppermute | solution.py:317
